TPU v7x, 768 devices: a whole 4x8x12 slice. The times are simulated.
768 devices in a mesh: section: 16 (over y_lo, x, core), fsdp: 48 (over z, y_hi).
Axes of the slice: x: 4, y: 8 (y_hi: 4, y_lo: 2; y = y_hi * 2 + y_lo), z: 12, core: 2. Of those that a mesh axis runs over, the one named last changes fastest.
Arguments:
- section_input: bfloat16 [16, 256, 12288], P('section', None, 'fsdp'), may hold values from -6 to 6
- stash_held: bfloat16 [16, 256, 12288], P('section', None, 'fsdp'), may hold values from -17 to 17
- upstream: bfloat16 [16, 256, 12288], P('section', None, 'fsdp'), may hold values from -6 to 6
- norm_gain: float32 [16, 12288], P('section', 'fsdp'), may hold values from 0.25 to 1.75
- out_weight: bfloat16 [16, 6144, 12288], P('section', None, 'fsdp'), may hold values from -0.078125 to 0.078125
Outputs:
- section_output: bfloat16 [16, 256, 12288], P('section', None, 'fsdp')
- stash_moved: bfloat16 [16, 256, 12288], P('section', None, 'fsdp')
- input_grad: bfloat16 [16, 256, 12288], P('section', None, 'fsdp')
All inputs are finite; a program needn't handle non-finite values.
Results may differ from a plain program's by a relative error of at most 0.012.
The roundings to bfloat16 on the way count: a program that leaves them out, or rounds other values in their place, can miss the bound.
Values may be sent and summed in bfloat16 or wider, within the bound.
A program may use at most 32 MiB of HBM per device.

v0:
```python
import jax
import jax.numpy as jnp
from jax import lax
from jax.sharding import PartitionSpec as P

D = 12288
HD = 128


EPSILON = 1e-05


def partner(value, axis, distance):
    mask = 2**distance
    pairs = [(source, source ^ mask) for source in range(lax.axis_size(axis))]
    return lax.ppermute(value, axis, pairs)


def attend(normed):
    tokens = normed.shape[0]
    paired = normed.reshape(tokens, normed.shape[1] // (2 * HD), 2, HD)
    queries = paired[:, :, 0]
    keyvals = paired[:, :, 1]
    shrink = HD ** (-0.5)
    scores = (
        jnp.einsum("qhd,khd->hqk", queries, keyvals, preferred_element_type=jnp.float32) * shrink
    )
    row_ids = lax.broadcasted_iota(jnp.int32, (tokens, tokens), 0)
    col_ids = lax.broadcasted_iota(jnp.int32, (tokens, tokens), 1)
    scores = jnp.where((row_ids >= col_ids)[None], scores, -1e30)
    probs = jax.nn.softmax(scores, axis=-1)
    weights = probs.astype(jnp.bfloat16)
    context = jnp.einsum("hqk,khd->qhd", weights, keyvals, preferred_element_type=jnp.float32)
    context = context.astype(jnp.bfloat16).reshape(tokens, -1)
    return (queries, keyvals, probs, weights, context)


def local(section_input, stash_held, upstream, norm_gain, out_weight):
    fresh = section_input[0]
    held = stash_held[0]
    grad_rows = upstream[0]
    gain_row = norm_gain[0]
    weight = out_weight[0]
    stacked = jnp.stack([fresh, held])
    sections = lax.axis_size("section")
    levels = sections.bit_length() - 1
    moved = stacked
    for level in range(levels):
        moved = partner(moved, "section", level)
    parked_out = moved[0]
    fetched = moved[1]
    fresh_f = fresh.astype(jnp.float32)
    held_f = fetched.astype(jnp.float32)
    totals_f, totals_b = lax.psum(
        (jnp.sum(fresh_f * fresh_f, axis=-1), jnp.sum(held_f * held_f, axis=-1)), "fsdp"
    )
    inverse_f = lax.rsqrt(totals_f / D + EPSILON)
    inverse_b = lax.rsqrt(totals_b / D + EPSILON)
    normed_f = (fresh_f * inverse_f[:, None] * gain_row[None]).astype(jnp.bfloat16)
    normed_b = (held_f * inverse_b[:, None] * gain_row[None]).astype(jnp.bfloat16)
    context_own = attend(normed_f)[4]
    weight_rows = weight
    projected = jnp.dot(
        lax.all_gather(context_own, "fsdp", axis=1, tiled=True),
        weight_rows,
        preferred_element_type=jnp.float32,
    )
    output = (fresh_f + projected).astype(jnp.bfloat16)
    queries, keyvals, probs, weights, unused = attend(normed_b)
    head_rows = context_own.shape[1]
    weight_rows = weight
    dcontext_t = lax.psum_scatter(
        lax.dot_general(
            weight_rows, grad_rows, (((1,), (1,)), ((), ())), preferred_element_type=jnp.float32
        ),
        "fsdp",
        scatter_dimension=0,
        tiled=True,
    )
    tokens = fresh.shape[0]
    dcontext = dcontext_t.T.astype(jnp.bfloat16).reshape(tokens, head_rows // HD, HD)
    dprob = jnp.einsum("qhd,khd->hqk", dcontext, keyvals, preferred_element_type=jnp.float32)
    dvalue = jnp.einsum("hqk,qhd->khd", weights, dcontext, preferred_element_type=jnp.float32)
    shrink = HD ** (-0.5)
    dscore = (probs * (dprob - jnp.sum(dprob * probs, axis=-1, keepdims=True)) * shrink).astype(
        jnp.bfloat16
    )
    dquery = jnp.einsum("hqk,khd->qhd", dscore, keyvals, preferred_element_type=jnp.float32)
    dkey = jnp.einsum("hqk,qhd->khd", dscore, queries, preferred_element_type=jnp.float32)
    dnormed = jnp.stack([dquery, dvalue + dkey], axis=2).reshape(tokens, -1)
    scaled = dnormed * gain_row[None]
    moment = lax.psum(jnp.sum(scaled * held_f, axis=-1), "fsdp")
    grad_in = grad_rows.astype(jnp.float32) + inverse_b[:, None] * scaled
    grad_in = grad_in - held_f * (inverse_b**3 * moment / D)[:, None]
    return (output[None], parked_out[None], grad_in.astype(jnp.bfloat16)[None])


def solution(mesh):
    placed = (
        P("section", None, "fsdp"),
        P("section", None, "fsdp"),
        P("section", None, "fsdp"),
        P("section", "fsdp"),
        P("section", None, "fsdp"),
    )
    return jax.shard_map(
        local,
        mesh=mesh,
        in_specs=placed,
        out_specs=(
            P("section", None, "fsdp"),
            P("section", None, "fsdp"),
            P("section", None, "fsdp"),
        ),
        check_vma=False,
    )
```

profile of v0, /device:TPU:6, one launch (start us, length us, event | category | flops | bytes accessed | tf_op | source)
XLA Modules:
  0.0 724.7 jit_solution(14603865346087881243)
XLA Ops:
  7.2 0.0 copy-start
  7.2 0.0 reduce-scatter.2.cloned.1.call-start
  7.2 1.8 copy-done
  9.1 4.6 fusion
  13.6 0.0 reduce-scatter.2.cloned.1.call-update
  13.7 0.0 all-gather.3.cloned.1.call-start
  13.7 0.8 copy-done.6
  14.5 0.1 copy.13
  14.7 0.1 copy.12
  14.8 1.9 collective-permute-start
  16.7 1.5 collective-permute-done
  18.2 2.7 collective-permute-start.1
  21.0 7.5 %collective-permute-done.1 = bf16[2,256,256]{1,2,0:T(8,128)(2,1)S(1)} collective-permute-done((bf16[2,256,256]{1,2,0:T(8,128)(2,1)S(1)}, bf16[2,256,256]{1,2,0:T(8,128)(2,1)S(1)}, u32[]{:S(2)}, u32[]{:S(2)}) %collective-permute-start.1) | collective-permute-done | bytes 262176 | tf_op jit(solution)/shard_map/ppermute | solution.py:16
  28.5 11.1 %collective-permute-start.2 = (bf16[2,256,256]{1,2,0:T(8,128)(2,1)S(1)}, bf16[2,256,256]{1,2,0:T(8,128)(2,1)}, u32[]{:S(2)}, u32[]{:S(2)}) collective-permute-start(bf16[2,256,256]{1,2,0:T(8,128)(2,1)S(1)} %collective-permute-done.1), channel_id=1, source_target_pairs={{0,192},{48,240},{96,288},{144,336},{192,0},{240,48},{288,96},{336... | collective-permute-start | bytes 786440 | tf_op jit(solution)/shard_map/ppermute | solution.py:16
  39.6 6.2 collective-permute-done.2
  45.8 1.9 collective-permute-start.3
  47.7 0.8 reshape.276
  48.5 0.7 fusion.24
  49.2 6.0 collective-permute-done.3
  55.2 0.8 fusion.39
  56.0 1.8 copy.15
  57.8 0.1 multiply_reduce_fusion.2
  57.8 125.6 %psum.22 = f32[256]{0:T(256)S(1)} all-reduce(f32[256]{0:T(256)S(1)} %multiply_reduce_fusion.2), channel_id=1, replica_groups=mesh['section'=16,'fsdp'=48] {'fsdp'}, use_global_device_ids=true, to_apply=%region_5.6 | all-reduce | flops 256 | bytes 2048 | tf_op jit(solution)/shard_map/psum | solution.py:54
  183.5 1.1 multiply_convert_fusion.1
  184.5 0.6 copy-done.4
  185.2 0.2 fusion.40
  185.4 0.7 copy-done.3
  186.1 0.6 fusion.29
  186.8 283.3 %reduce-scatter.2.cloned.1.call-done = f32[128,256]{1,0:T(8,128)} async-done(((f32[6144,256]{1,0:T(8,128)}), f32[128,256]{1,0:T(8,128)}) %reduce-scatter.2.cloned.1.call-update) | async-done | bytes 131088 | tf_op jit(solution)/shard_map/reduce_scatter | solution.py:72
  470.0 1.3 multiply_reduce_fusion.1
  471.3 1.0 multiply_convert_fusion
  472.3 1.0 convolution_bitcast_fusion
  473.4 1.2 fusion.31
  474.6 0.2 fusion.17
  474.9 1.0 multiply_reduce_fusion
  475.9 119.1 %all-reduce = (f32[256]{0:T(256)}, f32[256]{0:T(256)}) all-reduce(f32[256]{0:T(256)} %fusion.24, f32[256]{0:T(256)S(1)} %multiply_reduce_fusion), channel_id=1, replica_groups=mesh['section'=16,'fsdp'=48] {'fsdp'}, use_global_device_ids=true, to_apply=%region_1.0 | all-reduce | flops 512 | bytes 4096 | tf_op jit(solution)/shard_map/psum | solution.py:54
  595.0 0.7 fusion.37
  595.7 1.1 fusion.26
  596.8 0.2 fusion.41
  597.0 0.1 fusion.27
  597.1 0.8 fusion.23
  597.9 0.0 all-gather.3.cloned.1.call-update
  597.9 1.7 copy.14
  599.6 1.7 copy.16
  601.3 1.7 subtract_convert_fusion
  603.0 1.7 copy.17
  604.7 109.6 %all-gather.3.cloned.1.call-done = bf16[256,1,6144]{0,2,1:T(8,128)(2,1)} async-done(((bf16[256,1,128]{0,2,1:T(8,128)(2,1)}), bf16[256,1,6144]{0,2,1:T(8,128)(2,1)}) %all-gather.3.cloned.1.call-update) | async-done | bytes 3145744 | tf_op jit(solution)/shard_map/all_gather | solution.py:64
  714.3 3.6 fusion.18
  (14 shorter events, 0.1 us)
Async XLA Ops:
  7.2 1.9 copy-start
  7.2 462.8 %reduce-scatter.2.cloned.1.call-start = ((), (), s32[]{:S(2)}) async-start(), calls=%async_computation.1 | async-start | bytes 6422528 | tf_op jit(solution)/shard_map/reduce_scatter | solution.py:72
  13.6 0.9 copy-start.6
  13.6 1.0 copy-start.2
  13.6 169.8 %copy-start.7 = (f32[1,256]{1,0:T(1,128)S(1)}, f32[1,256]{1,0:T(1,128)}, u32[]{:S(2)}) copy-start(f32[1,256]{1,0:T(1,128)} %param.8) | copy-start | bytes 3076
  13.7 700.6 %all-gather.3.cloned.1.call-start = ((), (), s32[]{:S(2)}) async-start(), calls=%async_computation.2 | async-start | bytes 3211264 | tf_op jit(solution)/shard_map/all_gather | solution.py:64
  14.8 3.4 collective-permute-start
  18.2 10.2 %collective-permute-start.1 = (bf16[2,256,256]{1,2,0:T(8,128)(2,1)S(1)}, bf16[2,256,256]{1,2,0:T(8,128)(2,1)S(1)}, u32[]{:S(2)}, u32[]{:S(2)}) collective-permute-start(bf16[2,256,256]{1,2,0:T(8,128)(2,1)S(1)} %collective-permute-done), channel_id=1, source_target_pairs={{0,96},{48,144},{96,0},{144,48},{192,288},{240,336},{288,192},{336... | collective-permute-start | bytes 786440 | tf_op jit(solution)/shard_map/ppermute | solution.py:16
  28.5 17.3 %collective-permute-start.2 = (bf16[2,256,256]{1,2,0:T(8,128)(2,1)S(1)}, bf16[2,256,256]{1,2,0:T(8,128)(2,1)}, u32[]{:S(2)}, u32[]{:S(2)}) collective-permute-start(bf16[2,256,256]{1,2,0:T(8,128)(2,1)S(1)} %collective-permute-done.1), channel_id=1, source_target_pairs={{0,192},{48,240},{96,288},{144,336},{192,0},{240,48},{288,96},{336... | collective-permute-start | bytes 786440 | tf_op jit(solution)/shard_map/ppermute | solution.py:16
  45.8 9.4 %collective-permute-start.3 = (bf16[2,256,256]{1,2,0:T(8,128)(2,1)}, bf16[2,256,256]{1,2,0:T(8,128)(2,1)S(1)}, u32[]{:S(2)}, u32[]{:S(2)}) collective-permute-start(bf16[2,256,256]{1,2,0:T(8,128)(2,1)} %collective-permute-done.2), channel_id=1, source_target_pairs={{0,384},{48,432},{96,480},{144,528},{192,576},{240,624},{288,672},... | collective-permute-start | bytes 786440 | tf_op jit(solution)/shard_map/ppermute | solution.py:16
  55.2 419.5 %copy-start.1 = (bf16[2,256,256]{1,2,0:T(8,128)(2,1)}, bf16[2,256,256]{1,2,0:T(8,128)(2,1)S(1)}, u32[]{:S(2)}) copy-start(bf16[2,256,256]{1,2,0:T(8,128)(2,1)S(1)} %collective-permute-done.3) | copy-start | bytes 786436
  184.5 0.7 copy-start.4
  185.4 0.7 copy-start.3
  470.0 4.6 copy-start.5
Sparse Core Ops, SparseCore 0:
  13.8 456.1 reduce-scatter.1
  598.1 116.1 all-gather.2
where the time goes:
time: 726 us; the launch traced here: 725 us
  waiting for transfers between devices  414 us (57%)
  blocking collectives  245 us (34%)
  starting transfers between devices  17.7 us (2%)
  between operations  14.2 us (2%)
  matrix products  13.2 us (2%)
  local copies, waits for them, and re-layouts  11.9 us (2%)
  other arithmetic  8.9 us (1%)
    reduce_scatter x1, waiting for transfers between devices, local(): lax.psum_scatter(lax.dot_general(weight_rows, grad_rows, (((1,), (1,)), (...  283 us
    psum x2, blocking collectives, local(): lax.psum((jnp.sum(fresh_f * fresh_f, axis=-1), jnp.sum(held_f * held_f, a...  245 us
    all_gather x1, waiting for transfers between devices, local(): lax.all_gather(context_own, 'fsdp', axis=1, tiled=True)  110 us
    ppermute x4, waiting for transfers between devices, partner(): return lax.ppermute(value, axis, pairs)  21.2 us
    ppermute x4, starting transfers between devices, partner(): return lax.ppermute(value, axis, pairs)  17.7 us
  transfers between devices with their start and end apart: 6, of which 6 were waited for; matrix products, arithmetic and copies ran while one was open for 2% of the time, Pallas kernels for 0%

commit v1 on v0

v1 whole, which is shorter than its diff:
```python
import functools

import jax
import jax.numpy as jnp
from jax import lax
from jax.experimental import pallas as pl
from jax.experimental.pallas import tpu as pltpu
from jax.sharding import PartitionSpec as P

HD = 128
EPSILON = 1e-05
F32 = jnp.float32
BF16 = jnp.bfloat16
YS = 4


def dot(a, b):
    return lax.dot_general(a, b, (((1,), (0,)), ((), ())), preferred_element_type=F32)


def dot_t(a, b):
    return lax.dot_general(a, b, (((1,), (1,)), ((), ())), preferred_element_type=F32)


def columns(tile, row):
    halves = [
        jnp.transpose(jnp.broadcast_to(tile[row + i : row + i + 1], (HD, HD))) for i in range(2)
    ]
    half = jnp.concatenate(halves, axis=0)
    return jnp.concatenate([half, half], axis=1)


def token_sums(values):
    return jnp.sum(jnp.transpose(values), axis=0, keepdims=True)


def causal_probs(normed):
    queries, keyvals = normed[:, :HD], normed[:, HD:]
    scores = dot_t(queries, keyvals) * (HD**-0.5)
    rows = lax.broadcasted_iota(jnp.int32, scores.shape, 0)
    cols = lax.broadcasted_iota(jnp.int32, scores.shape, 1)
    scores = jnp.where(rows >= cols, scores, -1e30)
    shifted = jnp.exp(scores - jnp.max(scores, axis=-1, keepdims=True))
    return shifted / jnp.sum(shifted, axis=-1, keepdims=True)


def body(
    sections, zs, ys, fresh_hbm, held_hbm, up_hbm, gain_ref, w_hbm,
    out_ref, moved_ref, gin_ref,
    fresh_v, held_v, up_v, w_v, upt_v, fetched_v, acc_v, own_v, probs_v, normed_v,
    rs_out, rs_in, ys_out, ys_in, ctx_v,
    stat_v, stat_z, stat_y, stat_m, mom_v, mom_z, mom_y,
    load_sem, mir_send, mir_recv, rs_send, rs_recv, ys_send, ys_recv,
    yg_send, yg_recv, ag_send, ag_recv,
    sz_send, sz_recv, sy_send, sy_recv, mz_send, mz_recv, my_send, my_recv,
):
    width = zs * ys * 2 * HD
    sec = lax.axis_index("section")
    me = lax.axis_index("fsdp")
    z = me // ys
    y = me % ys
    half = zs // 2

    def at(dz, dy):
        return lax.rem(z + dz + zs, zs) * ys + lax.rem(y + dy + ys, ys)

    def remote(src, dst, send, recv, where):
        return pltpu.make_async_remote_copy(
            src_ref=src, dst_ref=dst, send_sem=send, recv_sem=recv,
            device_id=where, device_id_type=pl.DeviceIdType.MESH,
        )

    mirror = {"section": sections - 1 - sec}
    barrier = pltpu.get_barrier_semaphore()
    peers = [{"fsdp": at(d, 0)} for d in range(1, zs)] + [{"fsdp": at(0, d)} for d in range(1, ys)]
    peers.append(mirror)
    for peer in peers:
        pl.semaphore_signal(barrier, inc=1, device_id=peer, device_id_type=pl.DeviceIdType.MESH)
    loads = [
        pltpu.make_async_copy(src, dst, load_sem.at[i])
        for i, (src, dst) in enumerate(
            ((up_hbm, up_v), (w_hbm, w_v), (fresh_hbm, fresh_v), (held_hbm, held_v))
        )
    ]
    for load in loads:
        load.start()
    loads[0].wait()
    upt_v[...] = jnp.transpose(up_v[...].astype(F32)).astype(BF16)
    loads[1].wait()
    pl.semaphore_wait(barrier, len(peers))

    sent = []

    def partial(dz, j):
        row = at(dz, 1 + j) * HD
        return dot(w_v[pl.ds(pl.multiple_of(row, HD), HD), :], upt_v[...])

    def mine(way, j):
        return (j < ys // 2) == (way == 0)

    def rs_copy(way, k, j):
        return remote(
            rs_out.at[way, k, j], rs_in.at[way, k, j], rs_send.at[way, k, j],
            rs_recv.at[way, k, j], {"fsdp": at(1 - 2 * way, 0)},
        )

    def rs_step(k):
        for j in range(ys):
            for way in range(2):
                if k == 0 and not mine(way, j):
                    continue
                value = partial((1 - 2 * way) * (half - k), j)
                if k > 1 or (k == 1 and mine(way, j)):
                    rs_copy(way, k - 1, j).wait_recv()
                    value = value + rs_in[way, k - 1, j].astype(F32)
                rs_out[way, k, j] = value.astype(BF16)
                copy = rs_copy(way, k, j)
                copy.start()
                sent.append(copy)

    def ys_copy(j):
        return remote(
            ys_out.at[j], ys_in.at[j], ys_send.at[j], ys_recv.at[j], {"fsdp": at(0, 1 + j)}
        )

    def rs_last():
        for j in range(ys):
            value = partial(0, j)
            for way in range(2):
                rs_copy(way, half - 1, j).wait_recv()
                value = value + rs_in[way, half - 1, j].astype(F32)
            if j < ys - 1:
                ys_out[j] = value.astype(BF16)
                copy = ys_copy(j)
                copy.start()
                sent.append(copy)
            else:
                own_v[...] = value

    def z_sum_start(tile, landing, send, recv):
        for d in range(1, zs):
            copy = remote(
                tile, landing.at[d], send.at[d], recv.at[d], {"fsdp": at(d, 0)}
            )
            copy.start()
            sent.append(copy)

    def z_sum_end(tile, landing, send, recv):
        total = tile[...]
        for d in range(1, zs):
            remote(tile, landing.at[d], send.at[d], recv.at[d], {"fsdp": at(d, 0)}).wait_recv()
            total = total + landing[d]
        return total

    def y_sum_start(total, landing, send, recv):
        landing[0] = total
        for d in range(1, ys):
            copy = remote(
                landing.at[0], landing.at[d], send.at[d], recv.at[d], {"fsdp": at(0, d)}
            )
            copy.start()
            sent.append(copy)

    def y_sum_end(landing, send, recv):
        total = landing[0]
        for d in range(1, ys):
            remote(
                landing.at[0], landing.at[d], send.at[d], recv.at[d], {"fsdp": at(0, d)}
            ).wait_recv()
            total = total + landing[d]
        return total

    def yg_copy(d):
        return remote(
            ctx_v.at[me], ctx_v.at[me], yg_send.at[d], yg_recv.at[d], {"fsdp": at(0, d)}
        )

    def yg_wait(d):
        here = ctx_v.at[at(0, -d)]
        remote(here, here, yg_send.at[d], yg_recv.at[d], {"fsdp": at(0, d)}).wait_recv()

    def ag_copy(way, k, j):
        sign = 1 - 2 * way
        block = ctx_v.at[at(-sign * k, -j)]
        return remote(
            block, block, ag_send.at[way, k, j], ag_recv.at[way, k, j], {"fsdp": at(sign, 0)}
        )

    def ag_wait(way, k, j):
        sign = 1 - 2 * way
        block = ctx_v.at[at(-sign * (k + 1), -j)]
        remote(
            block, block, ag_send.at[way, k, j], ag_recv.at[way, k, j], {"fsdp": at(sign, 0)}
        ).wait_recv()

    def project(dz):
        first = lax.rem(z + dz + zs, zs) * ys
        total = acc_v[...]
        for pair in range(ys // 2):
            lhs = jnp.concatenate(
                [ctx_v[first + 2 * pair], ctx_v[first + 2 * pair + 1]], axis=1
            )
            row = (first + 2 * pair) * HD
            total = total + dot(lhs, w_v[pl.ds(pl.multiple_of(row, 2 * HD), 2 * HD), :])
        acc_v[...] = total

    def ag_step(k):
        for j in range(ys):
            for way in range(2):
                if k == 0 and j > 0 and way == 0:
                    yg_wait(j)
                if k > 0:
                    ag_wait(way, k - 1, j)
                if k == half - 1 and not mine(way, j):
                    continue
                copy = ag_copy(way, k, j)
                copy.start()
                sent.append(copy)
        if k == 0:
            project(0)
        else:
            project(-k)
            project(k)

    rs_step(0)
    loads[2].wait()
    loads[3].wait()
    for i, (src, dst) in enumerate(((held_v, fetched_v), (fresh_v, moved_ref))):
        copy = remote(src, dst, mir_send.at[i], mir_recv.at[i], mirror)
        copy.start()
        sent.append(copy)
    fresh = fresh_v[...].astype(F32)
    held = held_v[...].astype(F32)
    fresh_sq = token_sums(fresh * fresh)
    held_sq = token_sums(held * held)
    stat_v[...] = jnp.concatenate(
        [fresh_sq[:, :HD], fresh_sq[:, HD:], held_sq[:, :HD], held_sq[:, HD:],
         jnp.zeros((4, HD), F32)], axis=0
    )
    z_sum_start(stat_v, stat_z, sz_send, sz_recv)
    rs_step(1)
    y_sum_start(z_sum_end(stat_v, stat_z, sz_send, sz_recv), stat_y, sy_send, sy_recv)
    rs_step(2)
    inverse = lax.rsqrt(y_sum_end(stat_y, sy_send, sy_recv) / width + EPSILON)
    stat_m[0] = inverse
    copy = remote(stat_m.at[0], stat_m.at[1], mir_send.at[2], mir_recv.at[2], mirror)
    copy.start()
    sent.append(copy)
    gain = gain_ref[...]
    normed = (fresh_v[...].astype(F32) * columns(inverse, 0) * gain).astype(BF16)
    weights = causal_probs(normed).astype(BF16)
    ctx_v[me] = dot(weights, normed[:, HD:]).astype(BF16)
    for d in range(1, ys):
        copy = yg_copy(d)
        copy.start()
        sent.append(copy)
    acc_v[...] = fresh_v[...].astype(F32)
    rs_step(3)
    ag_step(0)
    for k in range(4, half):
        rs_step(k)
        ag_step(k - 3)
    rs_last()
    remote(held_v, fetched_v, mir_send.at[0], mir_recv.at[0], mirror).wait_recv()
    remote(stat_m.at[0], stat_m.at[1], mir_send.at[2], mir_recv.at[2], mirror).wait_recv()
    inverse_b = columns(stat_m[1], 2)
    normed_b = (fetched_v[...].astype(F32) * inverse_b * gain).astype(BF16)
    normed_v[...] = normed_b
    probs_v[...] = causal_probs(normed_b)
    done = half - 3
    ag_step(done)
    grad_t = own_v[...]
    for j in range(ys - 1):
        ys_copy(j).wait_recv()
        grad_t = grad_t + ys_in[j].astype(F32)
    dcontext = jnp.transpose(grad_t).astype(BF16)
    probs = probs_v[...]
    queries, keyvals = normed_v[:, :HD], normed_v[:, HD:]
    dprob = dot_t(dcontext, keyvals)
    dvalue = dot(jnp.transpose(probs).astype(BF16), dcontext)
    dscore = probs * (dprob - jnp.sum(dprob * probs, axis=-1, keepdims=True)) * (HD**-0.5)
    dquery = dot(dscore.astype(BF16), keyvals)
    dkey = dot(jnp.transpose(dscore).astype(BF16), queries)
    scaled = jnp.concatenate([dquery, dvalue + dkey], axis=1) * gain
    probs_v[...] = scaled
    moment = token_sums(scaled * fetched_v[...].astype(F32))
    mom_v[...] = jnp.concatenate(
        [moment[:, :HD], moment[:, HD:], jnp.zeros((6, HD), F32)], axis=0
    )
    z_sum_start(mom_v, mom_z, mz_send, mz_recv)
    ag_step(done + 1)
    y_sum_start(z_sum_end(mom_v, mom_z, mz_send, mz_recv), mom_y, my_send, my_recv)
    ag_step(done + 2)
    total = columns(y_sum_end(mom_y, my_send, my_recv), 0)
    inverse_b = columns(stat_m[1], 2)
    grad_in = up_v[...].astype(F32) + inverse_b * probs_v[...]
    grad_in = grad_in - fetched_v[...].astype(F32) * (
        inverse_b * inverse_b * inverse_b * total / width
    )
    gin_ref[...] = grad_in.astype(BF16)
    for j in range(ys):
        ag_wait(0 if mine(0, j) else 1, half - 1, j)
    project(half)
    out_ref[...] = acc_v[...].astype(BF16)
    remote(fresh_v, moved_ref, mir_send.at[1], mir_recv.at[1], mirror).wait_recv()
    for copy in sent:
        copy.wait_send()


def local(ys, sections, section_input, stash_held, upstream, norm_gain, out_weight):
    tokens, part = section_input.shape[1:]
    heads = out_weight.shape[1] // HD
    zs = heads // ys
    half = zs // 2
    dma = pltpu.SemaphoreType.DMA
    square = (tokens, part)
    whole = pl.BlockSpec(memory_space=pltpu.VMEM)
    anywhere = pl.BlockSpec(memory_space=pl.ANY)
    scratch = [
        pltpu.VMEM(square, BF16),
        pltpu.VMEM(square, BF16),
        pltpu.VMEM(square, BF16),
        pltpu.VMEM((heads * HD, part), BF16),
        pltpu.VMEM((part, tokens), BF16),
        pltpu.VMEM(square, BF16),
        pltpu.VMEM(square, F32),
        pltpu.VMEM((HD, tokens), F32),
        pltpu.VMEM((tokens, tokens), F32),
        pltpu.VMEM(square, BF16),
        pltpu.VMEM((2, half, ys, HD, tokens), BF16),
        pltpu.VMEM((2, half, ys, HD, tokens), BF16),
        pltpu.VMEM((ys, HD, tokens), BF16),
        pltpu.VMEM((ys, HD, tokens), BF16),
        pltpu.VMEM((heads, tokens, HD), BF16),
        pltpu.VMEM((8, HD), F32),
        pltpu.VMEM((zs, 8, HD), F32),
        pltpu.VMEM((ys, 8, HD), F32),
        pltpu.VMEM((2, 8, HD), F32),
        pltpu.VMEM((8, HD), F32),
        pltpu.VMEM((zs, 8, HD), F32),
        pltpu.VMEM((ys, 8, HD), F32),
        dma((4,)), dma((3,)), dma((3,)),
        dma((2, half, ys)), dma((2, half, ys)), dma((ys,)), dma((ys,)),
        dma((ys,)), dma((ys,)), dma((2, half, ys)), dma((2, half, ys)),
        dma((zs,)), dma((zs,)), dma((ys,)), dma((ys,)),
        dma((zs,)), dma((zs,)), dma((ys,)), dma((ys,)),
    ]
    result = jax.ShapeDtypeStruct(square, BF16)
    output, moved, grad_in = pl.pallas_call(
        functools.partial(body, sections, zs, ys),
        out_shape=(result, result, result),
        in_specs=[anywhere, anywhere, anywhere, whole, anywhere],
        out_specs=(whole, anywhere, whole),
        scratch_shapes=scratch,
        compiler_params=pltpu.CompilerParams(
            collective_id=0, has_side_effects=True, vmem_limit_bytes=48 * 1024 * 1024
        ),
        name="relay_tick",
    )(section_input[0], stash_held[0], upstream[0], norm_gain, out_weight[0])
    return output[None], moved[None], grad_in[None]


def solution(mesh):
    wide = P("section", None, "fsdp")
    return jax.shard_map(
        functools.partial(local, YS, mesh.shape["section"]),
        mesh=mesh,
        in_specs=(wide, wide, wide, P("section", "fsdp"), wide),
        out_specs=(wide, wide, wide),
        check_vma=False,
    )
```

time: 726 us -> 97.1 us (0.13)
  waiting for transfers between devices: 414 us -> 0 us
  blocking collectives: 245 us -> 0 us
  Pallas kernels: 0 us -> 89 us
  starting transfers between devices: 17.7 us -> 0 us
  between operations: 14.2 us -> 0.65 us
  matrix products: 13.2 us -> 0 us
  other arithmetic: 8.9 us -> 0 us
    reduce_scatter x1 -> x0, waiting for transfers between devices: 283 us -> none  [local(): lax.psum_scatter(lax.dot_general(weight_rows, grad_rows, (((1,), (1,)), (...]
    psum x2 -> x0, blocking collectives: 245 us -> none  [local(): lax.psum((jnp.sum(fresh_f * fresh_f, axis=-1), jnp.sum(held_f * held_f, a...]
    all_gather x1 -> x0, waiting for transfers between devices: 110 us -> none  [local(): lax.all_gather(context_own, 'fsdp', axis=1, tiled=True)]
    pallas_call x0 -> x1, Pallas kernels: none -> 89 us  [local(): pl.pallas_call(functools.partial(body, sections, zs, ys), out_shape=(resu...]
    ppermute x4 -> x0, waiting for transfers between devices: 21.2 us -> none  [partner(): return lax.ppermute(value, axis, pairs)]
    ppermute x4 -> x0, starting transfers between devices: 17.7 us -> none  [partner(): return lax.ppermute(value, axis, pairs)]
    dot_general x9 -> x0, matrix products: 13.2 us -> none  [the longest x1 4.58 us: local(): lax.dot_general(weight_rows, grad_rows, (((1,), (1,)), ((), ())), preferr...]
  transfers between devices with their start and end apart: 6 -> 0, of which waited for: 6 -> 0; matrix products, arithmetic and copies ran while one was open for 2% -> 0% of each run, Pallas kernels for 0% -> 0%
where the time goes in v1:
time: 97.1 us; the launch traced here: 96.9 us
  Pallas kernels  89 us (92%)
  local copies, waits for them, and re-layouts  7.24 us (7%)
    pallas_call x1, Pallas kernels, local(): pl.pallas_call(functools.partial(body, sections, zs, ys), out_shape=(resu...  89 us
    unnamed x13, local copies, waits for them, and re-layouts  7.24 us

profile of v1, /device:TPU:6, one launch (start us, length us, event | category | flops | bytes accessed | tf_op | source)
XLA Modules:
  0.0 96.9 jit_solution(8442297813160125785)
XLA Ops:
  0.6 0.0 copy-start
  0.6 1.9 %copy-done = bf16[1,6144,256]{2,1,0:T(8,128)(2,1)S(1)} copy-done((bf16[1,6144,256]{2,1,0:T(8,128)(2,1)S(1)}, bf16[1,6144,256]{2,1,0:T(8,128)(2,1)}, u32[]{:S(2)}) %copy-start) | copy-done | bytes 3145752
  2.5 0.0 copy-start.1
  2.5 0.9 copy-done.1
  3.4 0.0 copy-start.2
  3.4 0.9 copy-done.2
  4.3 0.0 copy-start.3
  4.3 0.9 copy-done.3
  5.2 0.0 copy-start.4
  5.2 0.7 copy-done.4
  5.9 89.0 %relay_tick.1 = (bf16[256,256]{1,0:T(8,128)(2,1)S(1)}, bf16[256,256]{1,0:T(8,128)(2,1)S(1)}, bf16[256,256]{1,0:T(8,128)(2,1)S(1)}) custom-call(bf16[256,256]{1,0:T(8,128)(2,1)S(1)} %bitcast.11, bf16[256,256]{1,0:T(8,128)(2,1)S(1)} %bitcast.12, bf16[256,256]{1,0:T(8,128)(2,1)S(1)} %bitcast.13, f32[1,256]{1,0:T(1,128)S(1)} %copy-done.4, ...), custom_call_target="tpu_custom_call" | custom-call | tf_op jit(solution)/shard_map/relay_tick/pallas_call | solution.py:349
  94.9 0.7 copy.11
  95.6 0.7 copy.12
  96.2 0.7 copy.13
Async XLA Ops:
  0.6 1.9 %copy-start = (bf16[1,6144,256]{2,1,0:T(8,128)(2,1)S(1)}, bf16[1,6144,256]{2,1,0:T(8,128)(2,1)}, u32[]{:S(2)}) copy-start(bf16[1,6144,256]{2,1,0:T(8,128)(2,1)} %param.9) | copy-start | bytes 9437188
  2.5 0.9 copy-start.1
  3.4 0.9 copy-start.2
  4.3 0.9 copy-start.3
  5.2 0.7 copy-start.4

commit v2 on v1

v2 whole, which is shorter than its diff:
```python
import functools

import jax
import jax.numpy as jnp
from jax import lax
from jax.experimental import pallas as pl
from jax.experimental.pallas import tpu as pltpu
from jax.sharding import PartitionSpec as P

HD = 128
EPSILON = 1e-05
F32 = jnp.float32
BF16 = jnp.bfloat16
YS = 4
SUM_FIRST = 80
GATHER_FIRST = 176


def dot(a, b):
    return lax.dot_general(a, b, (((1,), (0,)), ((), ())), preferred_element_type=F32)


def dot_t(a, b):
    return lax.dot_general(a, b, (((1,), (1,)), ((), ())), preferred_element_type=F32)


def columns(tile, row):
    halves = [
        jnp.transpose(jnp.broadcast_to(tile[row + i : row + i + 1], (HD, HD))) for i in range(2)
    ]
    half = jnp.concatenate(halves, axis=0)
    return jnp.concatenate([half, half], axis=1)


def token_sums(values):
    return jnp.sum(jnp.transpose(values), axis=0, keepdims=True)


def causal_probs(normed):
    queries, keyvals = normed[:, :HD], normed[:, HD:]
    scores = dot_t(queries, keyvals) * (HD**-0.5)
    rows = lax.broadcasted_iota(jnp.int32, scores.shape, 0)
    cols = lax.broadcasted_iota(jnp.int32, scores.shape, 1)
    scores = jnp.where(rows >= cols, scores, -1e30)
    shifted = jnp.exp(scores - jnp.max(scores, axis=-1, keepdims=True))
    return shifted / jnp.sum(shifted, axis=-1, keepdims=True)


def body(
    sections, zs, ys, fresh_hbm, held_hbm, up_hbm, gain_hbm, w_hbm,
    out_ref, moved_ref, gin_ref,
    fresh_v, held_v, up_v, gain_v, w_v, upt_v, fetched_v, acc_v, own_v, probs_v, normed_v,
    a_out, a_in, ay_out, ay_in, b0_out, b0_in, b1_out, b1_in, bz_out, bz_in, ctx_v,
    stat_v, stat_z, stat_y, stat_m, mom_v, mom_z, mom_y,
    load_sem, mir_send, mir_recv, a_send, a_recv, ay_send, ay_recv,
    b0_send, b0_recv, b1_send, b1_recv, bz_send, bz_recv,
    gy_send, gy_recv, ga_send, ga_recv, gz_send, gz_recv, h0_send, h0_recv, h1_send, h1_recv,
    sz_send, sz_recv, sy_send, sy_recv, mz_send, mz_recv, my_send, my_recv,
):
    width = zs * ys * 2 * HD
    tokens = fresh_v.shape[0]
    half = zs // 2
    fa, fb = SUM_FIRST, HD - SUM_FIRST
    ta, tb = GATHER_FIRST, tokens - GATHER_FIRST
    sec = lax.axis_index("section")
    me = lax.axis_index("fsdp")
    z = me // ys
    y = me % ys
    signs = (1, -1)

    def at(dz, dy):
        return lax.rem(z + dz + zs, zs) * ys + lax.rem(y + dy + ys, ys)

    def remote(src, dst, send, recv, where):
        return pltpu.make_async_remote_copy(
            src_ref=src, dst_ref=dst, send_sem=send, recv_sem=recv,
            device_id=where, device_id_type=pl.DeviceIdType.MESH,
        )

    mirror = {"section": sections - 1 - sec}
    barrier = pltpu.get_barrier_semaphore()
    peers = [{"fsdp": at(d, 0)} for d in range(1, zs)] + [{"fsdp": at(0, d)} for d in range(1, ys)]
    peers.append(mirror)
    quarter = w_v.shape[0] // 4
    pieces = [(w_hbm.at[pl.ds(i * quarter, quarter)], w_v.at[pl.ds(i * quarter, quarter)]) for i in range(4)]
    loads = [
        pltpu.make_async_copy(src, dst, load_sem.at[i])
        for i, (src, dst) in enumerate(
            [(fresh_hbm, fresh_v), (held_hbm, held_v), (up_hbm, up_v), *pieces, (gain_hbm, gain_v)]
        )
    ]
    for load in loads:
        load.start()
    for peer in peers:
        pl.semaphore_signal(barrier, inc=1, device_id=peer, device_id_type=pl.DeviceIdType.MESH)

    sent = []

    def start(copy):
        copy.start()
        sent.append(copy)

    def drain():
        for copy in sent:
            copy.wait_send()
        sent.clear()

    def partial(dz, dy, low, count):
        row = pl.multiple_of(at(dz, dy) * HD + low, 16)
        return dot(w_v[pl.ds(row, count), :], upt_v[...])

    def mine(way, j):
        return (j < ys // 2) == (way == 0)

    def a_copy(way, k, j):
        return remote(
            a_out.at[way, k, j], a_in.at[way, k, j], a_send.at[way, k, j], a_recv.at[way, k, j],
            {"fsdp": at(signs[way], 0)},
        )

    def a_step(k, j):
        for way in range(2):
            if k == 0 and not mine(way, j):
                continue
            value = partial(signs[way] * (half - k), 1 + j, 0, fa)
            if k > 1 or (k == 1 and mine(way, j)):
                a_copy(way, k - 1, j).wait_recv()
                value = value + a_in[way, k - 1, j].astype(F32)
            a_out[way, k, j] = value.astype(BF16)
            if k > 0:
                start(a_copy(way, k, j))

    def ay_copy(j):
        return remote(
            ay_out.at[j], ay_in.at[j], ay_send.at[j], ay_recv.at[j], {"fsdp": at(0, 1 + j)}
        )

    def a_last(j):
        value = partial(0, 1 + j, 0, fa)
        for way in range(2):
            a_copy(way, half - 1, j).wait_recv()
            value = value + a_in[way, half - 1, j].astype(F32)
        if j < ys - 1:
            ay_out[j] = value.astype(BF16)
            start(ay_copy(j))
        else:
            own_v[:fa] = value

    def of_way(d):
        return 0 if d > 0 else 1

    def b0_copy(d):
        i = d % zs
        return remote(
            b0_out.at[i], b0_in.at[i], b0_send.at[i], b0_recv.at[i],
            {"fsdp": at(0, signs[of_way(d)])},
        )

    def b1_copy(way, d):
        i = d % zs
        return remote(
            b1_out.at[way, i], b1_in.at[way, i], b1_send.at[way, i], b1_recv.at[way, i],
            {"fsdp": at(0, signs[way])},
        )

    def b1_step(d):
        for way in range(2):
            value = partial(d, signs[way], fa, fb)
            if of_way(d) == way:
                b0_copy(d).wait_recv()
                value = value + b0_in[d % zs].astype(F32)
            b1_out[way, d % zs] = value.astype(BF16)
            start(b1_copy(way, d))

    def y_total(d):
        value = partial(d, 0, fa, fb)
        for way in range(2):
            b1_copy(way, d).wait_recv()
            value = value + b1_in[way, d % zs].astype(F32)
        return value

    def bz_copy(way, k):
        return remote(
            bz_out.at[way, k], bz_in.at[way, k], bz_send.at[way, k], bz_recv.at[way, k],
            {"fsdp": at(signs[way], 0)},
        )

    def bz_step(k):
        for way in range(2):
            if k < way:
                continue
            value = y_total(signs[way] * (half - k))
            if k > way:
                bz_copy(way, k - 1).wait_recv()
                value = value + bz_in[way, k - 1].astype(F32)
            bz_out[way, k] = value.astype(BF16)
            start(bz_copy(way, k))

    def bz_last():
        value = y_total(0)
        for way in range(2):
            if half - 1 >= way:
                bz_copy(way, half - 1).wait_recv()
                value = value + bz_in[way, half - 1].astype(F32)
        own_v[fa:] = value

    def z_sum_start(tile, landing, send, recv):
        for d in range(1, zs):
            start(remote(tile, landing.at[d], send.at[d], recv.at[d], {"fsdp": at(d, 0)}))

    def z_sum_end(tile, landing, send, recv):
        total = tile[...]
        for d in range(1, zs):
            remote(tile, landing.at[d], send.at[d], recv.at[d], {"fsdp": at(d, 0)}).wait_recv()
            total = total + landing[d]
        return total

    def y_sum_start(total, landing, send, recv):
        landing[0] = total
        for d in range(1, ys):
            start(
                remote(landing.at[0], landing.at[d], send.at[d], recv.at[d], {"fsdp": at(0, d)})
            )

    def y_sum_end(landing, send, recv):
        total = landing[0]
        for d in range(1, ys):
            remote(
                landing.at[0], landing.at[d], send.at[d], recv.at[d], {"fsdp": at(0, d)}
            ).wait_recv()
            total = total + landing[d]
        return total

    def first(dz, dy):
        return ctx_v.at[at(dz, dy), pl.ds(0, ta)]

    def second(dz, dy):
        return ctx_v.at[at(dz, dy), pl.ds(ta, tb)]

    def gy_copy(d, block):
        return remote(block, block, gy_send.at[d], gy_recv.at[d], {"fsdp": at(0, d)})

    def ga_copy(way, k, j, block):
        return remote(
            block, block, ga_send.at[way, k, j], ga_recv.at[way, k, j], {"fsdp": at(signs[way], 0)}
        )

    def ga_step(k, j):
        if k == 0 and j > 0:
            gy_copy(j, first(0, -j)).wait_recv()
        for way in range(2):
            block = first(-signs[way] * k, -j)
            if k > 0:
                ga_copy(way, k - 1, j, block).wait_recv()
            if k < half - 1 or mine(way, j):
                start(ga_copy(way, k, j, block))

    def gz_copy(way, k, block):
        return remote(
            block, block, gz_send.at[way, k], gz_recv.at[way, k], {"fsdp": at(signs[way], 0)}
        )

    def h0_copy(way, d, block):
        i = d % zs
        return remote(
            block, block, h0_send.at[way, i], h0_recv.at[way, i], {"fsdp": at(0, signs[way])}
        )

    def h1_copy(d, block):
        i = d % zs
        return remote(
            block, block, h1_send.at[i], h1_recv.at[i], {"fsdp": at(0, signs[of_way(d)])}
        )

    def gz_step(s):
        for way in range(2):
            d = -signs[way] * s
            if (s == half and way == 0) or (s == 0 and way == 1):
                continue
            block = second(d, 0)
            if s > 0:
                gz_copy(way, s - 1, block).wait_recv()
            for to in range(2) if s == 0 else (way,):
                if s < half - 1 + to:
                    start(gz_copy(to, s, block))

    def h0_step(s):
        for d in both(s):
            for way in range(2):
                start(h0_copy(way, d, second(d, 0)))

    def both(s):
        return (s,) if s in (0, half) else (s, -s)

    def h1_step(s):
        for d in both(s):
            for way in range(2):
                block = second(d, -signs[way])
                h0_copy(way, d, block).wait_recv()
                if way == of_way(d):
                    start(h1_copy(d, block))

    def h1_end(s):
        for d in both(s):
            h1_copy(d, second(d, 2)).wait_recv()
            project(d, ta, tb)

    def project(dz, low, count):
        head = lax.rem(z + dz + zs, zs) * ys
        total = acc_v[low : low + count]
        for pair in range(ys // 2):
            lhs = jnp.concatenate(
                [ctx_v[head + 2 * pair + i, low : low + count] for i in range(2)], axis=1
            )
            row = pl.multiple_of((head + 2 * pair) * HD, 2 * HD)
            total = total + dot(lhs, w_v[pl.ds(row, 2 * HD), :])
        acc_v[low : low + count] = total

    def ga_slot(s, fresh_from=0):
        if s < half:
            for j in range(fresh_from, ys):
                ga_step(s, j)
        else:
            for j in range(ys):
                way = 0 if mine(0, j) else 1
                ga_copy(way, half - 1, j, first(half, -j)).wait_recv()
        for d in both(s):
            project(d, 0, ta)

    loads[0].wait()
    fresh = fresh_v[...].astype(F32)
    fresh_sq = token_sums(fresh * fresh)
    loads[1].wait()
    held = held_v[...].astype(F32)
    held_sq = token_sums(held * held)
    stats = jnp.concatenate(
        [fresh_sq[:, :HD], fresh_sq[:, HD:], held_sq[:, :HD], held_sq[:, HD:],
         jnp.zeros((4, HD), F32)], axis=0
    )
    loads[2].wait()
    upt_v[...] = jnp.transpose(up_v[...].astype(F32)).astype(BF16)
    pl.semaphore_wait(barrier, len(peers))
    y_sum_start(stats, stat_y, sy_send, sy_recv)
    for load in loads[3:]:
        load.wait()
    gain = gain_v[...]
    farthest = [half]
    for k in range(half - 1, 0, -1):
        farthest += [k, -k]
    farthest.append(0)
    for j in range(ys):
        a_step(0, j)
        start(a_copy(0 if mine(0, j) else 1, 0, j))
    for d in farthest:
        b0_out[d % zs] = partial(d, 2, fa, fb).astype(BF16)
        start(b0_copy(d))

    def stats_middle():
        stat_v[...] = y_sum_end(stat_y, sy_send, sy_recv)
        z_sum_start(stat_v, stat_z, sz_send, sz_recv)

    def mirror_start(i):
        src, dst = ((held_v, fetched_v), (fresh_v, moved_ref))[i]
        start(remote(src, dst, mir_send.at[i], mir_recv.at[i], mirror))

    def forward_attention():
        inverse = lax.rsqrt(z_sum_end(stat_v, stat_z, sz_send, sz_recv) / width + EPSILON)
        stat_m[0] = inverse
        start(remote(stat_m.at[0], stat_m.at[1], mir_send.at[2], mir_recv.at[2], mirror))
        values = fresh_v[...].astype(F32)
        normed = (values * columns(inverse, 0) * gain).astype(BF16)
        weights = causal_probs(normed).astype(BF16)
        ctx_v[me] = dot(weights, normed[:, HD:]).astype(BF16)
        acc_v[...] = values

    def backward_probs():
        remote(held_v, fetched_v, mir_send.at[0], mir_recv.at[0], mirror).wait_recv()
        remote(stat_m.at[0], stat_m.at[1], mir_send.at[2], mir_recv.at[2], mirror).wait_recv()
        normed_v[...] = (fetched_v[...].astype(F32) * columns(stat_m[1], 2) * gain).astype(BF16)
        probs_v[...] = causal_probs(normed_v[...])

    def backward_attention():
        grad_t = own_v[:fa]
        for j in range(ys - 1):
            ay_copy(j).wait_recv()
            grad_t = grad_t + ay_in[j].astype(F32)
        own_v[:fa] = grad_t
        dcontext = jnp.transpose(own_v[...]).astype(BF16)
        probs = probs_v[...]
        queries, keyvals = normed_v[:, :HD], normed_v[:, HD:]
        dprob = dot_t(dcontext, keyvals)
        dvalue = dot(jnp.transpose(probs).astype(BF16), dcontext)
        dscore = probs * (dprob - jnp.sum(dprob * probs, axis=-1, keepdims=True)) * (HD**-0.5)
        dquery = dot(dscore.astype(BF16), keyvals)
        dkey = dot(jnp.transpose(dscore).astype(BF16), queries)
        scaled = jnp.concatenate([dquery, dvalue + dkey], axis=1) * gain
        probs_v[...] = scaled
        moment = token_sums(scaled * fetched_v[...].astype(F32))
        mom_v[...] = jnp.concatenate(
            [moment[:, :HD], moment[:, HD:], jnp.zeros((6, HD), F32)], axis=0
        )
        z_sum_start(mom_v, mom_z, mz_send, mz_recv)

    def moment_middle():
        y_sum_start(z_sum_end(mom_v, mom_z, mz_send, mz_recv), mom_y, my_send, my_recv)

    def backward_end():
        total = columns(y_sum_end(mom_y, my_send, my_recv), 0)
        inverse = columns(stat_m[1], 2)
        grad_in = up_v[...].astype(F32) + inverse * probs_v[...]
        grad_in = grad_in - fetched_v[...].astype(F32) * (inverse**3 * total / width)
        gin_ref[...] = grad_in.astype(BF16)

    def gy_start():
        for d in range(1, ys):
            start(gy_copy(d, first(0, 0)))

    beside = {(k, j): [] for k in range(1, half) for j in range(ys)}

    def add(slot, step, what, *of):
        at_step = (slot, step) if slot < half else (half - 1, ys - 1)
        beside[at_step].append(functools.partial(what, *of))

    for i, d in enumerate(farthest[:3]):
        add(1, i + 1, b1_step, d)
    add(1, 3, stats_middle)
    for i, d in enumerate(farthest[3:7]):
        add(2, i, b1_step, d)
    add(2, 3, mirror_start, 0)
    for d in farthest[7:]:
        add(2, 3, b1_step, d)
    add(3, 0, forward_attention)
    add(3, 0, gz_step, 0)
    add(3, 2, gy_start)
    add(3, 3, ga_step, 0, 0)
    places = ((3, 3), (4, 1), (4, 3), (5, 1), (5, 3))
    for k in range(half - 1):
        add(*places[k], bz_step, k)
        add(*places[k], gz_step, k + 1)
    if half < 3:
        add(3, 3, gz_step, 2)
    for k in range(1, half):
        for j in range(ys):
            a_step(k, j)
            for what in beside[k, j]:
                what()
    for j in range(ys):
        a_last(j)
    h0_step(0)
    bz_step(half - 1)
    if half > 2:
        gz_step(half)
    bz_last()
    backward_probs()
    h0_step(1)
    ga_slot(0, 1)
    backward_attention()
    h0_turn = iter(range(2, half + 1))
    h1_turn = iter(range(half + 1))
    h1_begun = 0
    h1_done = 0
    for s in range(1, half):
        for count in range(2 if s == 2 else 1):
            h0_next = next(h0_turn, None)
            if h0_next is not None:
                h0_step(h0_next)
        ga_slot(s)
        if s == 1:
            mirror_start(1)
        for count in range(2 if s in (1, 3) else 1):
            h1_step(next(h1_turn))
            h1_begun += 1
        while h1_done < h1_begun - 2:
            h1_end(h1_done)
            h1_done += 1
        if s == min(2, half - 1):
            moment_middle()
        if s == min(4, half - 1):
            backward_end()
    for s in h0_turn:
        h0_step(s)
    drain()
    ga_slot(half)
    for s in h1_turn:
        h1_step(s)
    for s in range(h1_done, half + 1):
        h1_end(s)
    out_ref[...] = acc_v[...].astype(BF16)
    remote(fresh_v, moved_ref, mir_send.at[1], mir_recv.at[1], mirror).wait_recv()
    drain()


def local(ys, sections, section_input, stash_held, upstream, norm_gain, out_weight):
    tokens, part = section_input.shape[1:]
    heads = out_weight.shape[1] // HD
    zs = heads // ys
    half = zs // 2
    fb = HD - SUM_FIRST
    dma = pltpu.SemaphoreType.DMA
    square = (tokens, part)
    whole = pl.BlockSpec(memory_space=pltpu.VMEM)
    anywhere = pl.BlockSpec(memory_space=pl.ANY)
    buffers = [
        (square, BF16),
        (square, BF16),
        (square, BF16),
        ((1, part), F32),
        ((heads * HD, part), BF16),
        ((part, tokens), BF16),
        (square, BF16),
        (square, F32),
        ((HD, tokens), F32),
        ((tokens, tokens), F32),
        (square, BF16),
        ((2, half, ys, SUM_FIRST, tokens), BF16),
        ((2, half, ys, SUM_FIRST, tokens), BF16),
        ((ys, SUM_FIRST, tokens), BF16),
        ((ys, SUM_FIRST, tokens), BF16),
        ((zs, fb, tokens), BF16),
        ((zs, fb, tokens), BF16),
        ((2, zs, fb, tokens), BF16),
        ((2, zs, fb, tokens), BF16),
        ((2, half, fb, tokens), BF16),
        ((2, half, fb, tokens), BF16),
        ((heads, tokens, HD), BF16),
        ((8, HD), F32),
        ((zs, 8, HD), F32),
        ((ys, 8, HD), F32),
        ((2, 8, HD), F32),
        ((8, HD), F32),
        ((zs, 8, HD), F32),
        ((ys, 8, HD), F32),
    ]
    semaphores = [
        (8,), (3,), (3,), (2, half, ys), (2, half, ys), (ys,), (ys,),
        (zs,), (zs,), (2, zs), (2, zs), (2, half), (2, half),
        (ys,), (ys,), (2, half, ys), (2, half, ys), (2, half), (2, half),
        (2, zs), (2, zs), (zs,), (zs,),
        (zs,), (zs,), (ys,), (ys,), (zs,), (zs,), (ys,), (ys,),
    ]
    result = jax.ShapeDtypeStruct(square, BF16)
    output, moved, grad_in = pl.pallas_call(
        functools.partial(body, sections, zs, ys),
        out_shape=(result, result, result),
        in_specs=[pl.BlockSpec(memory_space=pltpu.HBM)] * 5,
        out_specs=(whole, anywhere, whole),
        scratch_shapes=[pltpu.VMEM(*b) for b in buffers] + [dma(s) for s in semaphores],
        compiler_params=pltpu.CompilerParams(
            collective_id=0, has_side_effects=True, vmem_limit_bytes=60 * 1024 * 1024
        ),
        name="relay_tick",
    )(section_input[0], stash_held[0], upstream[0], norm_gain, out_weight[0])
    return output[None], moved[None], grad_in[None]


def solution(mesh):
    wide = P("section", None, "fsdp")
    return jax.shard_map(
        functools.partial(local, YS, mesh.shape["section"]),
        mesh=mesh,
        in_specs=(wide, wide, wide, P("section", "fsdp"), wide),
        out_specs=(wide, wide, wide),
        check_vma=False,
    )
```

time: 97.1 us -> 93.6 us (0.964); the launches traced: 96.9 us -> 91.8 us
  local copies, waits for them, and re-layouts: 7.24 us -> 4.7 us
  Pallas kernels: 89 us -> 86.5 us
    unnamed x13 -> x3, local copies, waits for them, and re-layouts: 7.24 us -> 4.7 us
    pallas_call x1, Pallas kernels: 89 us -> 86.5 us  [local(): pl.pallas_call(functools.partial(body, sections, zs, ys), out_shape=(resu...]
where the time goes in v2:
time: 93.6 us; the launch traced here: 91.8 us
  Pallas kernels  86.5 us (92%)
  local copies, waits for them, and re-layouts  4.7 us (5%)
    pallas_call x1, Pallas kernels, local(): pl.pallas_call(functools.partial(body, sections, zs, ys), out_shape=(resu...  86.5 us
    unnamed x3, local copies, waits for them, and re-layouts  4.7 us

profile of v2, /device:TPU:6, one launch (start us, length us, event | category | flops | bytes accessed | tf_op | source)
XLA Modules:
  0.0 91.8 jit_solution(14830100230344002997)
XLA Ops:
  0.6 86.5 %relay_tick.1 = (bf16[256,256]{1,0:T(8,128)(2,1)}, bf16[256,256]{1,0:T(8,128)(2,1)}, bf16[256,256]{1,0:T(8,128)(2,1)}) custom-call(bf16[256,256]{1,0:T(8,128)(2,1)} %bitcast.11, bf16[256,256]{1,0:T(8,128)(2,1)} %bitcast.12, bf16[256,256]{1,0:T(8,128)(2,1)} %bitcast.13, f32[1,256]{1,0:T(1,128)} %gain_hbm.1, bf16[6144,256]{1,0:T(8,128)(2,1)} %bitcast.7), custom_call_target="tpu_custom_call" | custom-call | tf_op jit(solution)/shard_map/relay_tick/pallas_call | solution.py:542
  87.1 1.6 %copy.11 = bf16[1,256,256]{2,1,0:T(8,128)(2,1)} copy(bf16[1,256,256]{2,1,0:T(8,128)(2,1)} %bitcast.10) | data formatting | bytes 262144
  88.7 1.6 %copy.12 = bf16[1,256,256]{2,1,0:T(8,128)(2,1)} copy(bf16[1,256,256]{2,1,0:T(8,128)(2,1)} %bitcast.9) | data formatting | bytes 262144
  90.2 1.6 %copy.13 = bf16[1,256,256]{2,1,0:T(8,128)(2,1)} copy(bf16[1,256,256]{2,1,0:T(8,128)(2,1)} %bitcast.8) | data formatting | bytes 262144

commit v3 on v2

--- a/solution.py
+++ b/solution.py
@@ -12,8 +12,8 @@
 F32 = jnp.float32
 BF16 = jnp.bfloat16
 YS = 4
-SUM_FIRST = 80
-GATHER_FIRST = 176
+SUM_FIRST = 96
+GATHER_FIRST = 192
 
 
 def dot(a, b):

time: 93.6 us -> 93.6 us (level); the launches traced: 91.8 us -> 92.9 us
  Pallas kernels: 86.5 us -> 87.6 us
    pallas_call x1, Pallas kernels: 86.5 us -> 87.6 us  [local(): pl.pallas_call(functools.partial(body, sections, zs, ys), out_shape=(resu...]
where the time goes in v3:
time: 93.6 us; the launch traced here: 92.9 us
  Pallas kernels  87.6 us (94%)
  local copies, waits for them, and re-layouts  4.7 us (5%)
    pallas_call x1, Pallas kernels, local(): pl.pallas_call(functools.partial(body, sections, zs, ys), out_shape=(resu...  87.6 us
    unnamed x3, local copies, waits for them, and re-layouts  4.7 us

profile of v3, /device:TPU:6, one launch (start us, length us, event | category | flops | bytes accessed | tf_op | source)
XLA Modules:
  0.0 92.9 jit_solution(15158218288069714533)
XLA Ops:
  0.6 87.6 %relay_tick.1 = (bf16[256,256]{1,0:T(8,128)(2,1)}, bf16[256,256]{1,0:T(8,128)(2,1)}, bf16[256,256]{1,0:T(8,128)(2,1)}) custom-call(bf16[256,256]{1,0:T(8,128)(2,1)} %bitcast.11, bf16[256,256]{1,0:T(8,128)(2,1)} %bitcast.12, bf16[256,256]{1,0:T(8,128)(2,1)} %bitcast.13, f32[1,256]{1,0:T(1,128)} %gain_hbm.1, bf16[6144,256]{1,0:T(8,128)(2,1)} %bitcast.7), custom_call_target="tpu_custom_call" | custom-call | tf_op jit(solution)/shard_map/relay_tick/pallas_call | solution.py:542
  88.2 1.6 %copy.11 = bf16[1,256,256]{2,1,0:T(8,128)(2,1)} copy(bf16[1,256,256]{2,1,0:T(8,128)(2,1)} %bitcast.10) | data formatting | bytes 262144
  89.8 1.6 %copy.12 = bf16[1,256,256]{2,1,0:T(8,128)(2,1)} copy(bf16[1,256,256]{2,1,0:T(8,128)(2,1)} %bitcast.9) | data formatting | bytes 262144
  91.4 1.6 %copy.13 = bf16[1,256,256]{2,1,0:T(8,128)(2,1)} copy(bf16[1,256,256]{2,1,0:T(8,128)(2,1)} %bitcast.8) | data formatting | bytes 262144
